TPU v7x, 32 devices: a whole 2x2x4 slice. The times are simulated.
32 devices in a mesh: groups: 2 (over y), ctx: 16 (over z, x, core).
Axes of the slice: x: 2, y: 2, z: 4, core: 2. Of those that a mesh axis runs over, the one named last changes fastest.
Arguments:
- queries: bfloat16 [4096, 512], P(('groups', 'ctx')), parts along dimension 0, may hold values from -150 to 150
- keys: bfloat16 [4096, 512], P(('groups', 'ctx')), parts along dimension 0, may hold values from -6 to 6
- values: bfloat16 [4096, 512], P(('groups', 'ctx')), parts along dimension 0, may hold values from -6 to 6
- cotangent: bfloat16 [4096, 512], P(('groups', 'ctx')), parts along dimension 0, may hold values from -6 to 6
Outputs:
- attended: bfloat16 [4096, 512], P(('groups', 'ctx')), parts along dimension 0
- query_grad: bfloat16 [4096, 512], P(('groups', 'ctx')), parts along dimension 0
- key_grad: bfloat16 [4096, 512], P(('groups', 'ctx')), parts along dimension 0
- value_grad: bfloat16 [4096, 512], P(('groups', 'ctx')), parts along dimension 0
There are 2 independent parts, one for each index of `groups`. A program takes and returns all parts, laid end to end along the dimension named above; each array names one. Nothing has to cross between parts.
All inputs are finite; a program needn't handle non-finite values.
Results may differ from a plain program's by a relative error of at most 0.022.
Values may be sent and summed in bfloat16 or wider, within the bound.
A program may use at most 64 MiB of HBM per device.

v0:
```python
import jax
import jax.numpy as jnp
from jax import lax
from jax.sharding import PartitionSpec as P

HEADS = 4
HEAD_DIM = 128
BLOCK = 128


ROOT_HALF = 0.70710678


def swapped(value, axis, stride):
    mask = 2**stride
    pairs = [(source, source ^ mask) for source in range(lax.axis_size(axis))]
    return lax.ppermute(value, axis, pairs)


def pool_rows(pairs):
    widened = pairs.astype(jnp.float32).reshape(pairs.shape[0] // 2, 2, pairs.shape[1])
    return ((widened[:, 0] + widened[:, 1]) * ROOT_HALF).astype(jnp.bfloat16)


def attend_sets(queries, cotangent, pair_sets, groups):
    row_count = queries.shape[0]
    model_cols = queries.shape[1]
    set_width = pair_sets[0].shape[1]
    score_scale = HEAD_DIM ** (-0.5)
    attended_heads = []
    query_heads = []
    key_heads = [[] for member in pair_sets]
    value_heads = [[] for member in pair_sets]
    for head_index in range(HEADS):
        low_col = head_index * HEAD_DIM
        q_head = queries[:, low_col : low_col + HEAD_DIM]
        d_head = cotangent[:, low_col : low_col + HEAD_DIM]
        key_parts = []
        value_parts = []
        score_list = []
        for pair_set, group_size in zip(pair_sets, groups):
            key_part = pair_set[:, :, low_col : low_col + HEAD_DIM]
            value_part = pair_set[:, :, model_cols + low_col : model_cols + low_col + HEAD_DIM]
            key_parts.append(key_part)
            value_parts.append(value_part)
            q_group = q_head.reshape(row_count // group_size, group_size, HEAD_DIM)
            score_list.append(
                jnp.einsum(
                    "gsd,gkd->gsk", q_group, key_part, preferred_element_type=jnp.float32
                ).reshape(row_count, set_width)
            )
        scores = jnp.stack(score_list, axis=0) * score_scale
        peak = jnp.max(scores, axis=(0, 2))
        weights = jnp.exp(scores - peak[None, :, None])
        probs = weights / jnp.sum(weights, axis=(0, 2))[None, :, None]
        probs_low = probs.astype(jnp.bfloat16)
        output = jnp.zeros((row_count, HEAD_DIM), jnp.float32)
        dprob_list = []
        for set_index in range(len(pair_sets)):
            group_size = groups[set_index]
            p_group = probs_low[set_index].reshape(row_count // group_size, group_size, set_width)
            output = output + jnp.einsum(
                "gsk,gkd->gsd", p_group, value_parts[set_index], preferred_element_type=jnp.float32
            ).reshape(row_count, HEAD_DIM)
            d_group = d_head.reshape(row_count // group_size, group_size, HEAD_DIM)
            dprob_list.append(
                jnp.einsum(
                    "gsd,gkd->gsk",
                    d_group,
                    value_parts[set_index],
                    preferred_element_type=jnp.float32,
                ).reshape(row_count, set_width)
            )
        attended = output.astype(jnp.bfloat16)
        delta = jnp.sum(d_head.astype(jnp.float32) * attended.astype(jnp.float32), axis=1)
        dprobs = jnp.stack(dprob_list, axis=0)
        dscores = (score_scale * probs * (dprobs - delta[None, :, None])).astype(jnp.bfloat16)
        query_total = jnp.zeros((row_count, HEAD_DIM), jnp.float32)
        for set_index in range(len(pair_sets)):
            group_size = groups[set_index]
            s_group = dscores[set_index].reshape(row_count // group_size, group_size, set_width)
            p_group = probs_low[set_index].reshape(row_count // group_size, group_size, set_width)
            q_group = q_head.reshape(row_count // group_size, group_size, HEAD_DIM)
            d_group = d_head.reshape(row_count // group_size, group_size, HEAD_DIM)
            query_total = query_total + jnp.einsum(
                "gsk,gkd->gsd", s_group, key_parts[set_index], preferred_element_type=jnp.float32
            ).reshape(row_count, HEAD_DIM)
            key_heads[set_index].append(
                jnp.einsum("gsk,gsd->gkd", s_group, q_group, preferred_element_type=jnp.float32)
            )
            value_heads[set_index].append(
                jnp.einsum("gsk,gsd->gkd", p_group, d_group, preferred_element_type=jnp.float32)
            )
        attended_heads.append(attended)
        query_heads.append(query_total)
    set_grads = [
        jnp.concatenate(key_heads[set_index] + value_heads[set_index], axis=2)
        for set_index in range(len(pair_sets))
    ]
    return (
        jnp.concatenate(attended_heads, axis=1),
        jnp.concatenate(query_heads, axis=1),
        set_grads,
    )


def upper_member(position, bit_number):
    return position // (1 << bit_number) % 2 == 1


def per_device(queries, keys, values, cotangent):
    tok_count, model_cols = queries.shape
    ctx_count = lax.axis_size("ctx")
    position = lax.axis_index("ctx")
    block_count = tok_count // BLOCK
    local_levels = block_count.bit_length() - 1
    all_levels = (block_count * ctx_count).bit_length() - 1
    pair_level = [jnp.concatenate([keys, values], axis=1)]
    for level_index in range(1, all_levels):
        pair_level.append(pool_rows(pair_level[-1]))
    pair_sets = [pair_level[0].reshape(block_count, BLOCK, 2 * model_cols)]
    groups = [BLOCK]
    far_pairs = [None for level_index in range(local_levels, all_levels)]
    own_pairs = pair_level[local_levels]
    for level_index in range(local_levels, all_levels):
        bit_number = level_index - local_levels
        received = swapped(own_pairs, "ctx", bit_number)
        far_pairs[bit_number] = received
        if level_index + 1 < all_levels:
            upper = upper_member(position, bit_number)
            joined = jnp.where(
                upper,
                jnp.concatenate([received, own_pairs], axis=0),
                jnp.concatenate([own_pairs, received], axis=0),
            )
            own_pairs = pool_rows(joined)
    for level_index in range(local_levels, all_levels):
        pair_sets.append(far_pairs[level_index - local_levels].reshape(1, BLOCK, 2 * model_cols))
        groups.append(tok_count)
    attended, query_grad, set_grads = attend_sets(queries, cotangent, pair_sets, groups)
    grads = [
        jnp.zeros((tok_count >> level_index, 2 * model_cols), jnp.float32)
        for level_index in range(all_levels)
    ]
    grads[0] = set_grads[0].reshape(tok_count, 2 * model_cols)
    far_grads = [
        set_grads[1 + level_index].reshape(BLOCK, 2 * model_cols)
        for level_index in range(local_levels, all_levels)
    ]
    carried = None
    for level_index in reversed(range(local_levels, all_levels)):
        bit_number = level_index - local_levels
        outgoing = far_grads[bit_number]
        if carried is None:
            kept = jnp.zeros((BLOCK, 2 * model_cols), jnp.float32)
        else:
            spread = jnp.repeat(carried, 2, axis=0) * ROOT_HALF
            lower_half = spread[:BLOCK]
            upper_half = spread[BLOCK:]
            upper = upper_member(position, bit_number)
            kept = jnp.where(upper, upper_half, lower_half)
            outgoing = outgoing + jnp.where(upper, lower_half, upper_half)
        carried = kept + swapped(outgoing, "ctx", bit_number)
    grads[local_levels] = grads[local_levels] + carried
    for level_index in range(all_levels - 1, 0, -1):
        grads[level_index - 1] = (
            grads[level_index - 1] + jnp.repeat(grads[level_index], 2, axis=0) * ROOT_HALF
        )
    key_grad = grads[0][:, :model_cols].astype(jnp.bfloat16)
    value_grad = grads[0][:, model_cols:].astype(jnp.bfloat16)
    return (attended, query_grad.astype(jnp.bfloat16), key_grad, value_grad)


def solution(mesh):
    placed = (
        P(("groups", "ctx"), None),
        P(("groups", "ctx"), None),
        P(("groups", "ctx"), None),
        P(("groups", "ctx"), None),
    )
    return jax.shard_map(
        per_device,
        mesh=mesh,
        in_specs=placed,
        out_specs=(
            P(("groups", "ctx"), None),
            P(("groups", "ctx"), None),
            P(("groups", "ctx"), None),
            P(("groups", "ctx"), None),
        ),
        check_vma=False,
    )
```

profile of v0, /device:TPU:1, one launch (start us, length us, event | category | flops | bytes accessed | tf_op | source)
XLA Modules:
  0.0 136.8 jit_solution(2825736501846280894)
XLA Ops:
  0.6 0.9 constant_dynamic-update-slice_fusion.1
  7.4 1.1 fusion.107
  8.5 1.8 %reshape.960 = f32[128,2,1024]{2,1,0:T(2,128)S(1)} reshape(f32[256,1024]{1,0:T(8,128)} %fusion.107) | data formatting | bytes 2097152 | tf_op jit(solution)/shard_map/convert_element_type | solution.py:21
  11.2 2.1 %collective-permute-start.1 = (bf16[128,1024]{1,0:T(8,128)(2,1)S(1)}, bf16[128,1024]{1,0:T(8,128)(2,1)S(1)}, u32[]{:S(2)}, u32[]{:S(2)}) collective-permute-start(bf16[128,1024]{1,0:T(8,128)(2,1)S(1)} %bitcast.825), channel_id=1, source_target_pairs={{0,2},{1,3},{2,0},{3,1},{4,6},{5,7},{6,4},{7,5},{8,10},{9,11},{10,... | collective-permute-start | bytes 786440 | tf_op jit(solution)/shard_map/ppermute | solution.py:17
  17.0 2.3 %collective-permute-done.1 = bf16[128,1024]{1,0:T(8,128)(2,1)S(1)} collective-permute-done((bf16[128,1024]{1,0:T(8,128)(2,1)S(1)}, bf16[128,1024]{1,0:T(8,128)(2,1)S(1)}, u32[]{:S(2)}, u32[]{:S(2)}) %collective-permute-start.1) | collective-permute-done | bytes 262176 | tf_op jit(solution)/shard_map/ppermute | solution.py:17
  19.5 1.6 %reshape.961 = f32[128,2,1024]{2,1,0:T(2,128)} reshape(f32[256,1024]{1,0:T(8,128)S(1)} %fusion.108) | data formatting | bytes 2097152 | tf_op jit(solution)/shard_map/convert_element_type | solution.py:21
  21.1 2.5 %fusion.112 = bf16[128,1,1024]{2,1,0:T(2,128)(2,1)S(1)} fusion(f32[128,2,1024]{2,1,0:T(2,128)} %reshape.961), kind=kLoop, calls=%fused_computation.220 | loop fusion | flops 393216 | bytes 1310720 | tf_op jit(solution)/shard_map/convert_element_type | solution.py:22
  23.6 1.3 collective-permute-start.2
  28.6 1.6 %collective-permute-done.2 = bf16[128,1024]{1,0:T(8,128)(2,1)S(1)} collective-permute-done((bf16[128,1024]{1,0:T(8,128)(2,1)S(1)}, bf16[128,1024]{1,0:T(8,128)(2,1)S(1)}, u32[]{:S(2)}, u32[]{:S(2)}) %collective-permute-start.2) | collective-permute-done | bytes 262176 | tf_op jit(solution)/shard_map/ppermute | solution.py:17
  31.1 1.6 %reshape.962 = f32[128,2,1024]{2,1,0:T(2,128)} reshape(f32[256,1024]{1,0:T(8,128)S(1)} %fusion.109) | data formatting | bytes 2097152 | tf_op jit(solution)/shard_map/convert_element_type | solution.py:21
  32.7 2.5 %fusion.113 = bf16[128,1,1024]{2,1,0:T(2,128)(2,1)S(1)} fusion(f32[128,2,1024]{2,1,0:T(2,128)} %reshape.962), kind=kLoop, calls=%fused_computation.221 | loop fusion | flops 393216 | bytes 1310720 | tf_op jit(solution)/shard_map/convert_element_type | solution.py:22
  35.3 2.0 %collective-permute-start.3 = (bf16[128,1024]{1,0:T(8,128)(2,1)S(1)}, bf16[128,1024]{1,0:T(8,128)(2,1)S(1)}, u32[]{:S(2)}, u32[]{:S(2)}) collective-permute-start(bf16[128,1024]{1,0:T(8,128)(2,1)S(1)} %bitcast.845), channel_id=1, source_target_pairs={{0,8},{1,9},{2,10},{3,11},{4,12},{5,13},{6,14},{7,15},{8,0},{9,1},... | collective-permute-start | bytes 786440 | tf_op jit(solution)/shard_map/ppermute | solution.py:17
  38.8 10.7 %collective-permute-done.3 = bf16[128,1024]{1,0:T(8,128)(2,1)S(1)} collective-permute-done((bf16[128,1024]{1,0:T(8,128)(2,1)S(1)}, bf16[128,1024]{1,0:T(8,128)(2,1)S(1)}, u32[]{:S(2)}, u32[]{:S(2)}) %collective-permute-start.3) | collective-permute-done | bytes 262176 | tf_op jit(solution)/shard_map/ppermute | solution.py:17
  60.6 0.9 multiply_reduce_fusion.6
  63.9 0.9 multiply_reduce_fusion.7
  77.1 18.6 %collective-permute-done.4 = f32[128,1024]{0,1:T(8,128)S(1)} collective-permute-done((f32[128,1024]{0,1:T(8,128)S(1)}, f32[128,1024]{0,1:T(8,128)S(1)}, u32[]{:S(2)}, u32[]{:S(2)}) %collective-permute-start.4) | collective-permute-done | bytes 524320 | tf_op jit(solution)/shard_map/ppermute | solution.py:17
  96.9 1.9 %bitcast_add_fusion.2 = f32[128,1024]{0,1:T(8,128)} fusion(f32[128,1024]{0,1:T(8,128)S(1)} %copy.44, f32[1,128,1024]{1,2,0:T(8,128)} %copy-done.8), kind=kLoop, calls=%fused_computation.214 | loop fusion | flops 131072 | bytes 1572864 | tf_op jit(solution)/shard_map/add | solution.py:162
  99.7 1.6 %fusion.103 = bf16[128,128]{0,1:T(8,128)(2,1)} fusion(f32[128,128]{0,1:T(8,128)S(1)} %copy-done.21, f32[128,128]{0,1:T(8,128)S(1)} %copy-done.22, f32[128,128]{0,1:T(8,128)S(1)} %convolution_add_fusion.1, bf16[1,128,1024]{2,1,0:T(8,128)(2,1)S(1)} %bitcast.789, bf16[5,128,128]{1,2,0:T(8,128)(2,1)} %copy-done.4), kind=kOutput, calls=%fused_computation.199 | convolution fusion | flops 4259840 | bytes 294912 | tf_op jit(solution)/shard_map/gsk,gkd->gsd/dot_general | solution.py:85
  102.4 8.4 %collective-permute-done.5 = f32[128,1024]{0,1:T(8,128)} collective-permute-done((f32[128,1024]{0,1:T(8,128)}, f32[128,1024]{0,1:T(8,128)}, u32[]{:S(2)}, u32[]{:S(2)}) %collective-permute-start.5) | collective-permute-done | bytes 524320 | tf_op jit(solution)/shard_map/ppermute | solution.py:17
  110.8 1.1 add_multiply_fusion.1
  113.1 1.9 %bitcast_add_fusion.1 = f32[128,1024]{0,1:T(8,128)} fusion(f32[128,1024]{0,1:T(8,128)S(1)} %copy.48, f32[1,128,1024]{1,2,0:T(8,128)} %copy-done.7), kind=kLoop, calls=%fused_computation.213 | loop fusion | flops 131072 | bytes 1572864 | tf_op jit(solution)/shard_map/add | solution.py:162
  118.1 8.1 %collective-permute-done.6 = f32[128,1024]{0,1:T(8,128)} collective-permute-done((f32[128,1024]{0,1:T(8,128)}, f32[128,1024]{0,1:T(8,128)}, u32[]{:S(2)}, u32[]{:S(2)}) %collective-permute-start.6) | collective-permute-done | bytes 524320 | tf_op jit(solution)/shard_map/ppermute | solution.py:17
  126.2 1.1 add_multiply_fusion
  129.4 3.6 %collective-permute-start.7 = (f32[128,1024]{0,1:T(8,128)S(1)}, f32[128,1024]{0,1:T(8,128)S(1)}, u32[]{:S(2)}, u32[]{:S(2)}) collective-permute-start(f32[128,1024]{0,1:T(8,128)S(1)} %bitcast_add_fusion), channel_id=1, source_target_pairs={{0,1},{1,0},{2,3},{3,2},{4,5},{5,4},{6,7},{7,6},{8,9},{9,8},{10,11... | collective-permute-start | bytes 1572872 | tf_op jit(solution)/shard_map/ppermute | solution.py:17
  (250 shorter events, 55.2 us)
Async XLA Ops:
  1.6 5.8 %collective-permute-start = (bf16[128,1024]{1,0:T(8,128)(2,1)S(1)}, bf16[128,1024]{1,0:T(8,128)(2,1)S(1)}, u32[]{:S(2)}, u32[]{:S(2)}) collective-permute-start(bf16[128,1024]{1,0:T(8,128)(2,1)S(1)} %constant_dynamic-update-slice_fusion), channel_id=1, source_target_pairs={{0,1},{1,0},{2,3},{3,2},{4,5},{5,4},{6,7},{7,6},{8,9},{9,8},{10,11... | collective-permute-start | bytes 786440 | tf_op jit(solution)/shard_map/ppermute | solution.py:17
  11.2 8.1 %collective-permute-start.1 = (bf16[128,1024]{1,0:T(8,128)(2,1)S(1)}, bf16[128,1024]{1,0:T(8,128)(2,1)S(1)}, u32[]{:S(2)}, u32[]{:S(2)}) collective-permute-start(bf16[128,1024]{1,0:T(8,128)(2,1)S(1)} %bitcast.825), channel_id=1, source_target_pairs={{0,2},{1,3},{2,0},{3,1},{4,6},{5,7},{6,4},{7,5},{8,10},{9,11},{10,... | collective-permute-start | bytes 786440 | tf_op jit(solution)/shard_map/ppermute | solution.py:17
  23.6 6.6 %collective-permute-start.2 = (bf16[128,1024]{1,0:T(8,128)(2,1)S(1)}, bf16[128,1024]{1,0:T(8,128)(2,1)S(1)}, u32[]{:S(2)}, u32[]{:S(2)}) collective-permute-start(bf16[128,1024]{1,0:T(8,128)(2,1)S(1)} %bitcast.827), channel_id=1, source_target_pairs={{0,4},{1,5},{2,6},{3,7},{4,0},{5,1},{6,2},{7,3},{8,12},{9,13},{10,... | collective-permute-start | bytes 786440 | tf_op jit(solution)/shard_map/ppermute | solution.py:17
  35.2 2.1 %copy-start.3 = (bf16[128,1024]{1,0:T(8,128)(2,1)S(1)}, bf16[128,1024]{1,0:T(8,128)(2,1)}, u32[]{:S(2)}) copy-start(bf16[128,1024]{1,0:T(8,128)(2,1)} %copy-done.2) | copy-start | bytes 786436
  35.2 2.7 %copy-start.13 = (f32[5,128,128]{1,2,0:T(8,128)S(1)}, f32[5,128,128]{1,2,0:T(8,128)}, u32[]{:S(2)}) copy-start(f32[5,128,128]{1,2,0:T(8,128)} %fusion.44) | copy-start | bytes 983044
  35.2 3.4 %copy-start.14 = (f32[5,128,128]{1,2,0:T(8,128)S(1)}, f32[5,128,128]{1,2,0:T(8,128)}, u32[]{:S(2)}) copy-start(f32[5,128,128]{1,2,0:T(8,128)} %fusion.65) | copy-start | bytes 983044
  35.3 14.1 %collective-permute-start.3 = (bf16[128,1024]{1,0:T(8,128)(2,1)S(1)}, bf16[128,1024]{1,0:T(8,128)(2,1)S(1)}, u32[]{:S(2)}, u32[]{:S(2)}) collective-permute-start(bf16[128,1024]{1,0:T(8,128)(2,1)S(1)} %bitcast.845), channel_id=1, source_target_pairs={{0,8},{1,9},{2,10},{3,11},{4,12},{5,13},{6,14},{7,15},{8,0},{9,1},... | collective-permute-start | bytes 786440 | tf_op jit(solution)/shard_map/ppermute | solution.py:17
  55.1 19.4 %copy-start.4 = (bf16[5,128,128]{1,2,0:T(8,128)(2,1)}, bf16[5,128,128]{1,2,0:T(8,128)(2,1)S(1)}, u32[]{:S(2)}) copy-start(bf16[5,128,128]{1,2,0:T(8,128)(2,1)S(1)} %multiply_convert_fusion) | copy-start | bytes 491524
  69.3 2.0 %copy-start.9 = (f32[1,128,1024]{1,2,0:T(8,128)}, f32[1,128,1024]{1,2,0:T(8,128)S(1)}, u32[]{:S(2)}) copy-start(f32[1,128,1024]{1,2,0:T(8,128)S(1)} %fusion.34) | copy-start | bytes 1572868
  70.8 24.8 %collective-permute-start.4 = (f32[128,1024]{0,1:T(8,128)S(1)}, f32[128,1024]{0,1:T(8,128)S(1)}, u32[]{:S(2)}, u32[]{:S(2)}) collective-permute-start(f32[128,1024]{0,1:T(8,128)S(1)} %bitcast.846), channel_id=1, source_target_pairs={{0,8},{1,9},{2,10},{3,11},{4,12},{5,13},{6,14},{7,15},{8,0},{9,1},... | collective-permute-start | bytes 1572872 | tf_op jit(solution)/shard_map/ppermute | solution.py:17
  72.6 1.7 %copy-start.8 = (f32[1,128,1024]{1,2,0:T(8,128)}, f32[1,128,1024]{1,2,0:T(8,128)S(1)}, u32[]{:S(2)}) copy-start(f32[1,128,1024]{1,2,0:T(8,128)S(1)} %fusion.16) | copy-start | bytes 1572868
  74.1 3.0 %copy-start.7 = (f32[1,128,1024]{1,2,0:T(8,128)}, f32[1,128,1024]{1,2,0:T(8,128)S(1)}, u32[]{:S(2)}) copy-start(f32[1,128,1024]{1,2,0:T(8,128)S(1)} %fusion.8) | copy-start | bytes 1572868
  75.4 1.7 %copy-start.5 = (f32[1,128,1024]{1,2,0:T(8,128)}, f32[1,128,1024]{1,2,0:T(8,128)S(1)}, u32[]{:S(2)}) copy-start(f32[1,128,1024]{1,2,0:T(8,128)S(1)} %fusion.1) | copy-start | bytes 1572868
  98.8 12.0 %collective-permute-start.5 = (f32[128,1024]{0,1:T(8,128)}, f32[128,1024]{0,1:T(8,128)}, u32[]{:S(2)}, u32[]{:S(2)}) collective-permute-start(f32[128,1024]{0,1:T(8,128)} %bitcast_add_fusion.2), channel_id=1, source_target_pairs={{0,4},{1,5},{2,6},{3,7},{4,0},{5,1},{6,2},{7,3},{8,12},{9,13},{10,... | collective-permute-start | bytes 1572872 | tf_op jit(solution)/shard_map/ppermute | solution.py:17
  99.6 1.6 %copy-start.23 = (f32[128,128]{0,1:T(8,128)S(1)}, f32[128,128]{0,1:T(8,128)}, u32[]{:S(2)}) copy-start(f32[128,128]{0,1:T(8,128)} %fusion.140) | copy-start | bytes 196612
  99.7 1.6 %copy-start.24 = (f32[128,128]{0,1:T(8,128)S(1)}, f32[128,128]{0,1:T(8,128)}, u32[]{:S(2)}) copy-start(f32[128,128]{0,1:T(8,128)} %fusion.139) | copy-start | bytes 196612
  113.1 2.0 %copy-start.26 = (bf16[128,128]{0,1:T(8,128)(2,1)S(1)}, bf16[128,128]{0,1:T(8,128)(2,1)}, u32[]{:S(2)}) copy-start(bf16[128,128]{0,1:T(8,128)(2,1)} %get-tuple-element.29) | copy-start | bytes 98308
  113.1 2.0 %copy-start.27 = (bf16[128,128]{0,1:T(8,128)(2,1)S(1)}, bf16[128,128]{0,1:T(8,128)(2,1)}, u32[]{:S(2)}) copy-start(bf16[128,128]{0,1:T(8,128)(2,1)} %get-tuple-element.31) | copy-start | bytes 98308
  113.1 2.0 %copy-start.28 = (bf16[128,128]{0,1:T(8,128)(2,1)S(1)}, bf16[128,128]{0,1:T(8,128)(2,1)}, u32[]{:S(2)}) copy-start(bf16[128,128]{0,1:T(8,128)(2,1)} %get-tuple-element.33) | copy-start | bytes 98308
  113.1 2.0 %copy-start.29 = (bf16[128,128]{0,1:T(8,128)(2,1)S(1)}, bf16[128,128]{0,1:T(8,128)(2,1)}, u32[]{:S(2)}) copy-start(bf16[128,128]{0,1:T(8,128)(2,1)} %get-tuple-element.35) | copy-start | bytes 98308
  115.1 11.1 %collective-permute-start.6 = (f32[128,1024]{0,1:T(8,128)}, f32[128,1024]{0,1:T(8,128)}, u32[]{:S(2)}, u32[]{:S(2)}) collective-permute-start(f32[128,1024]{0,1:T(8,128)} %bitcast_add_fusion.1), channel_id=1, source_target_pairs={{0,2},{1,3},{2,0},{3,1},{4,6},{5,7},{6,4},{7,5},{8,10},{9,11},{10,... | collective-permute-start | bytes 1572872 | tf_op jit(solution)/shard_map/ppermute | solution.py:17
  129.3 3.7 %copy-start.30 = (bf16[128,128]{0,1:T(8,128)(2,1)S(1)}, bf16[128,128]{0,1:T(8,128)(2,1)}, u32[]{:S(2)}) copy-start(bf16[128,128]{0,1:T(8,128)(2,1)} %fusion.103) | copy-start | bytes 98308
  129.3 4.4 %copy-start.10 = (f32[1,128,1024]{1,2,0:T(8,128)S(1)}, f32[1,128,1024]{1,2,0:T(8,128)}, u32[]{:S(2)}) copy-start(f32[1,128,1024]{1,2,0:T(8,128)} %copy-done.9) | copy-start | bytes 1572868
  129.4 5.8 %collective-permute-start.7 = (f32[128,1024]{0,1:T(8,128)S(1)}, f32[128,1024]{0,1:T(8,128)S(1)}, u32[]{:S(2)}, u32[]{:S(2)}) collective-permute-start(f32[128,1024]{0,1:T(8,128)S(1)} %bitcast_add_fusion), channel_id=1, source_target_pairs={{0,1},{1,0},{2,3},{3,2},{4,5},{5,4},{6,7},{7,6},{8,9},{9,8},{10,11... | collective-permute-start | bytes 1572872 | tf_op jit(solution)/shard_map/ppermute | solution.py:17
  (15 other events, 13.5 us)
where the time goes:
time: 138 us; the launch traced here: 137 us
  waiting for transfers between devices  49.7 us (36%)
  matrix products  41.4 us (30%)
  local copies, waits for them, and re-layouts  19.4 us (14%)
  other arithmetic  15.7 us (11%)
  starting transfers between devices  9.18 us (7%)
  between operations  1.45 us (1%)
    ppermute x8, waiting for transfers between devices, swapped(): return lax.ppermute(value, axis, pairs)  49.7 us
    dot_general x20, matrix products, attend_sets(): jnp.einsum('gsk,gkd->gsd', s_group, key_parts[set_index], preferred_eleme...  11.9 us
    dot_general x20, matrix products, attend_sets(): jnp.einsum('gsd,gkd->gsk', d_group, value_parts[set_index], preferred_ele...  10.5 us
    ppermute x8, starting transfers between devices, swapped(): return lax.ppermute(value, axis, pairs)  9.18 us
    unnamed x75, local copies, waits for them, and re-layouts  8.84 us
    dot_general x20, matrix products, attend_sets(): jnp.einsum('gsk,gkd->gsd', p_group, value_parts[set_index], preferred_ele...  6.8 us
    convert_element_type x3, other arithmetic, pool_rows(): return ((widened[:, 0] + widened[:, 1]) * ROOT_HALF).astype(jnp.bfloat16)  5.74 us
    convert_element_type x3, local copies, waits for them, and re-layouts, pool_rows(): pairs.astype(jnp.float32).reshape(pairs.shape[0] // 2, 2, pairs.shape[1])  5.04 us
  transfers between devices with their start and end apart: 8, of which 6 were waited for; matrix products, arithmetic and copies ran while one was open for 20% of the time, Pallas kernels for 0%

commit v1 on v0

--- a/solution.py
+++ b/solution.py
@@ -1,6 +1,10 @@
+import functools
+
 import jax
 import jax.numpy as jnp
 from jax import lax
+from jax.experimental import pallas as pl
+from jax.experimental.pallas import tpu as pltpu
 from jax.sharding import PartitionSpec as P
 
 HEADS = 4
@@ -108,7 +112,7 @@
     return position // (1 << bit_number) % 2 == 1
 
 
-def per_device(queries, keys, values, cotangent):
+def per_device_chained(queries, keys, values, cotangent):
     tok_count, model_cols = queries.shape
     ctx_count = lax.axis_size("ctx")
     position = lax.axis_index("ctx")
@@ -171,6 +175,320 @@
     return (attended, query_grad.astype(jnp.bfloat16), key_grad, value_grad)
 
 
+def chunk_slot(level, member):
+    return (1 << level) - 2 + member
+
+
+def contract(left, right, left_dim, right_dim):
+    return lax.dot_general(
+        left, right, (((left_dim,), (right_dim,)), ((), ())), preferred_element_type=jnp.float32
+    )
+
+
+def exchange_kernel(
+    levels,
+    q_ref,
+    k_ref,
+    v_ref,
+    d_ref,
+    att_ref,
+    dq_ref,
+    dk_ref,
+    dv_ref,
+    wide,
+    pooled,
+    q_all,
+    d_all,
+    kv_all,
+    grad_out,
+    grad_in,
+    near_out,
+    near_in,
+    att_out,
+    dq_out,
+    spread,
+    pool_send,
+    pool_recv,
+    near_send,
+    near_recv,
+    grad_send,
+    grad_recv,
+    back_send,
+    back_recv,
+):
+    me = lax.axis_index("ctx")
+    count = 1 << levels
+    core = lax.rem(me, 2)
+    sibling = me + 1 - 2 * core
+    half = 2 * HEAD_DIM
+    own_cols = pl.ds(pl.multiple_of(core * half, half), half)
+    sib_cols = pl.ds(pl.multiple_of(half - core * half, half), half)
+
+    def remote(src, dst, send, recv, target):
+        return pltpu.make_async_remote_copy(
+            src_ref=src,
+            dst_ref=dst,
+            send_sem=send,
+            recv_sem=recv,
+            device_id={"ctx": target},
+            device_id_type=pl.DeviceIdType.MESH,
+        )
+
+    barrier = pltpu.get_barrier_semaphore()
+    for step in range(1, count):
+        other = lax.rem(me + step, count)
+        pl.semaphore_signal(
+            barrier, inc=1, device_id={"ctx": other}, device_id_type=pl.DeviceIdType.MESH
+        )
+
+    for c in range(2):
+        for part in range(4):
+            src = k_ref if part < 2 else v_ref
+            low_col = c * half + part % 2 * HEAD_DIM
+            wide[c * 4 + part] = src[:, low_col : low_col + HEAD_DIM].astype(jnp.float32)
+    for level in range(1, levels):
+        rows = BLOCK >> level
+        base = BLOCK - 2 * rows
+        for c in range(2):
+            for part in range(4):
+                column = wide.at[c * 4 + part]
+                even = column[pl.ds(0, rows, stride=2), :]
+                odd = column[pl.ds(1, rows, stride=2), :]
+                low = ((even + odd) * ROOT_HALF).astype(jnp.bfloat16)
+                pooled[c, base : base + rows, part * HEAD_DIM : (part + 1) * HEAD_DIM] = low
+                if level + 1 < levels:
+                    column[0:rows, :] = low.astype(jnp.float32)
+    pl.semaphore_wait(barrier, count - 1)
+
+    def pool_copy(level, member):
+        rows = BLOCK >> level
+        base = BLOCK - 2 * rows
+        size = 1 << level
+        mine = lax.rem(me, size)
+        group = lax.div(me, size)
+        partner = group + 1 - 2 * lax.rem(group, 2)
+        return remote(
+            pooled.at[member % 2, pl.ds(base, rows), :],
+            kv_all.at[pl.ds(pl.multiple_of(BLOCK * (level + 1) + mine * rows, rows), rows), :],
+            pool_send.at[chunk_slot(level, member)],
+            pool_recv.at[chunk_slot(level, 0) + mine],
+            partner * size + member,
+        )
+
+    def pool_arrival(level, member):
+        rows = BLOCK >> level
+        base = BLOCK - 2 * rows
+        return remote(
+            pooled.at[0, pl.ds(base, rows), :],
+            kv_all.at[pl.ds(BLOCK * (level + 1) + member * rows, rows), :],
+            pool_send.at[chunk_slot(level, member)],
+            pool_recv.at[chunk_slot(level, member)],
+            sibling,
+        )
+
+    own_rows = pl.ds(pl.multiple_of(core * BLOCK, BLOCK), BLOCK)
+    sib_rows = pl.ds(pl.multiple_of(BLOCK - core * BLOCK, BLOCK), BLOCK)
+    near = [
+        remote(src.at[:, sib_cols], dst, near_send.at[i], near_recv.at[i], sibling)
+        for i, (src, dst) in enumerate(
+            [
+                (q_ref, q_all.at[own_rows, :]),
+                (k_ref, kv_all.at[own_rows, pl.ds(0, half)]),
+                (v_ref, kv_all.at[own_rows, pl.ds(half, half)]),
+                (d_ref, d_all.at[own_rows, :]),
+            ]
+        )
+    ]
+    pool_copies = [
+        pool_copy(level, member) for level in reversed(range(1, levels)) for member in range(1 << level)
+    ]
+    for copy in near:
+        copy.start()
+    for copy in pool_copies:
+        copy.start()
+    q_all[own_rows, :] = q_ref[:, own_cols]
+    d_all[own_rows, :] = d_ref[:, own_cols]
+    kv_all[own_rows, 0:half] = k_ref[:, own_cols]
+    kv_all[own_rows, half : 2 * half] = v_ref[:, own_cols]
+    for copy in near:
+        copy.wait_recv()
+
+    segments = [(0, 2 * BLOCK)] + [(BLOCK * (level + 1), BLOCK) for level in range(1, levels)]
+    score_scale = HEAD_DIM ** (-0.5)
+    scores = [[], []]
+    dprobs = [[], []]
+    q_heads = [q_all[:, h * HEAD_DIM : (h + 1) * HEAD_DIM] for h in range(2)]
+    d_heads = [d_all[:, h * HEAD_DIM : (h + 1) * HEAD_DIM] for h in range(2)]
+
+    def k_part(index, h):
+        low, rows = segments[index]
+        return kv_all[low : low + rows, h * HEAD_DIM : (h + 1) * HEAD_DIM]
+
+    def v_part(index, h):
+        low, rows = segments[index]
+        return kv_all[low : low + rows, half + h * HEAD_DIM : half + (h + 1) * HEAD_DIM]
+
+    for index in range(levels):
+        if index > 0:
+            for member in range(1 << index):
+                pool_arrival(index, member).wait_recv()
+        for h in range(2):
+            scores[h].append(contract(q_heads[h], k_part(index, h), 1, 1) * score_scale)
+            dprobs[h].append(contract(d_heads[h], v_part(index, h), 1, 1))
+
+    def grad_copy(level, member):
+        rows = BLOCK >> level
+        size = 1 << level
+        mine = lax.rem(me, size)
+        group = lax.div(me, size)
+        partner = group + 1 - 2 * lax.rem(group, 2)
+        return remote(
+            grad_out.at[level - 1, pl.ds(member * rows, rows), :],
+            grad_in.at[level - 1, pl.ds(pl.multiple_of(mine * rows, rows), rows), :],
+            grad_send.at[chunk_slot(level, member)],
+            grad_recv.at[chunk_slot(level, 0) + mine],
+            partner * size + member,
+        )
+
+    def grad_arrival(level, member):
+        rows = BLOCK >> level
+        return remote(
+            grad_out.at[level - 1, pl.ds(member * rows, rows), :],
+            grad_in.at[level - 1, pl.ds(member * rows, rows), :],
+            grad_send.at[chunk_slot(level, member)],
+            grad_recv.at[chunk_slot(level, member)],
+            sibling,
+        )
+
+    near_grads = []
+    for h in range(2):
+        low_col = h * HEAD_DIM
+        peak = jnp.max(scores[h][0], axis=1, keepdims=True)
+        for part in scores[h][1:]:
+            peak = jnp.maximum(peak, jnp.max(part, axis=1, keepdims=True))
+        weights = [jnp.exp(part - peak) for part in scores[h]]
+        total = jnp.sum(weights[0], axis=1, keepdims=True)
+        for part in weights[1:]:
+            total = total + jnp.sum(part, axis=1, keepdims=True)
+        inverse = 1.0 / total
+        probs = [part * inverse for part in weights]
+        probs_low = [part.astype(jnp.bfloat16) for part in probs]
+        output = contract(probs_low[0], v_part(0, h), 1, 0)
+        for index in range(1, levels):
+            output = output + contract(probs_low[index], v_part(index, h), 1, 0)
+        attended = output.astype(jnp.bfloat16)
+        att_out[:, low_col : low_col + HEAD_DIM] = attended
+        delta = jnp.sum(
+            d_heads[h].astype(jnp.float32) * attended.astype(jnp.float32), axis=1, keepdims=True
+        )
+        dscores = [
+            (score_scale * part * (dpart - delta)).astype(jnp.bfloat16)
+            for part, dpart in zip(probs, dprobs[h])
+        ]
+        for index in range(1, levels):
+            grad_out[index - 1, :, low_col : low_col + HEAD_DIM] = contract(
+                dscores[index], q_heads[h], 0, 0
+            ).astype(jnp.bfloat16)
+            grad_out[index - 1, :, half + low_col : half + low_col + HEAD_DIM] = contract(
+                probs_low[index], d_heads[h], 0, 0
+            ).astype(jnp.bfloat16)
+        near_grads.append((dscores, probs_low))
+    grad_copies = [
+        grad_copy(level, member) for level in reversed(range(1, levels)) for member in range(1 << level)
+    ]
+    for copy in grad_copies:
+        copy.start()
+    for h in range(2):
+        low_col = h * HEAD_DIM
+        dscores, probs_low = near_grads[h]
+        near_out[:, low_col : low_col + HEAD_DIM] = contract(dscores[0], q_heads[h], 0, 0).astype(jnp.bfloat16)
+        near_out[:, half + low_col : half + low_col + HEAD_DIM] = contract(
+            probs_low[0], d_heads[h], 0, 0
+        ).astype(jnp.bfloat16)
+        query_total = contract(dscores[0], k_part(0, h), 1, 0)
+        for index in range(1, levels):
+            query_total = query_total + contract(dscores[index], k_part(index, h), 1, 0)
+        dq_out[:, low_col : low_col + HEAD_DIM] = query_total.astype(jnp.bfloat16)
+    back = [
+        remote(near_out.at[sib_rows, :], near_in.at[core], back_send.at[0], back_recv.at[0], sibling),
+        remote(att_out.at[sib_rows, :], att_ref.at[:, own_cols], back_send.at[1], back_recv.at[1], sibling),
+        remote(dq_out.at[sib_rows, :], dq_ref.at[:, own_cols], back_send.at[2], back_recv.at[2], sibling),
+    ]
+    for copy in back:
+        copy.start()
+    near_in[core] = near_out[own_rows, :]
+    att_ref[:, own_cols] = att_out[own_rows, :]
+    dq_ref[:, own_cols] = dq_out[own_rows, :]
+    for level in reversed(range(1, levels)):
+        for member in range(1 << level):
+            grad_arrival(level, member).wait_recv()
+    back[0].wait_recv()
+    for c in range(2):
+        carried = None
+        for level in reversed(range(1, levels)):
+            rows = BLOCK >> level
+            for member in range(c, 1 << level, 2):
+                part = grad_in[level - 1, member * rows : (member + 1) * rows, :].astype(jnp.float32)
+                carried = part if carried is None else carried + part
+            carried = carried * ROOT_HALF
+            for part in range(4):
+                column = spread.at[part]
+                piece = carried[:, part * HEAD_DIM : (part + 1) * HEAD_DIM]
+                column[pl.ds(0, rows, stride=2), :] = piece
+                column[pl.ds(1, rows, stride=2), :] = piece
+            carried = jnp.concatenate([spread[part, 0 : 2 * rows, :] for part in range(4)], axis=1)
+        carried = carried + near_in[c].astype(jnp.float32)
+        low = carried.astype(jnp.bfloat16)
+        dk_ref[:, c * half : (c + 1) * half] = low[:, :half]
+        dv_ref[:, c * half : (c + 1) * half] = low[:, half:]
+    for copy in back[1:]:
+        copy.wait_recv()
+    for copy in near + pool_copies + grad_copies + back:
+        copy.wait_send()
+
+
+def per_device(queries, keys, values, cotangent):
+    tok_count, model_cols = queries.shape
+    levels = lax.axis_size("ctx").bit_length() - 1
+    if tok_count != BLOCK or levels < 2 or BLOCK >> (levels - 1) < 16:
+        return per_device_chained(queries, keys, values, cotangent)
+    chunks = (1 << levels) - 2
+    half = model_cols // 2
+    flat = jax.ShapeDtypeStruct((tok_count, model_cols), jnp.bfloat16)
+    vmem = pl.BlockSpec(memory_space=pltpu.VMEM)
+    return pl.pallas_call(
+        functools.partial(exchange_kernel, levels),
+        out_shape=(flat, flat, flat, flat),
+        in_specs=[vmem] * 4,
+        out_specs=(vmem,) * 4,
+        scratch_shapes=[
+            pltpu.VMEM((8, BLOCK, HEAD_DIM), jnp.float32),
+            pltpu.VMEM((2, BLOCK, model_cols), jnp.bfloat16),
+            pltpu.VMEM((2 * BLOCK, half), jnp.bfloat16),
+            pltpu.VMEM((2 * BLOCK, half), jnp.bfloat16),
+            pltpu.VMEM((BLOCK * (levels + 1), model_cols), jnp.bfloat16),
+            pltpu.VMEM((levels - 1, BLOCK, model_cols), jnp.bfloat16),
+            pltpu.VMEM((levels - 1, BLOCK, model_cols), jnp.bfloat16),
+            pltpu.VMEM((2 * BLOCK, model_cols), jnp.bfloat16),
+            pltpu.VMEM((2, BLOCK, model_cols), jnp.bfloat16),
+            pltpu.VMEM((2 * BLOCK, half), jnp.bfloat16),
+            pltpu.VMEM((2 * BLOCK, half), jnp.bfloat16),
+            pltpu.VMEM((4, BLOCK, HEAD_DIM), jnp.float32),
+            pltpu.SemaphoreType.DMA((chunks,)),
+            pltpu.SemaphoreType.DMA((chunks,)),
+            pltpu.SemaphoreType.DMA((4,)),
+            pltpu.SemaphoreType.DMA((4,)),
+            pltpu.SemaphoreType.DMA((chunks,)),
+            pltpu.SemaphoreType.DMA((chunks,)),
+            pltpu.SemaphoreType.DMA((3,)),
+            pltpu.SemaphoreType.DMA((3,)),
+        ],
+        compiler_params=pltpu.CompilerParams(
+            collective_id=0, has_side_effects=True, vmem_limit_bytes=32 * 1024 * 1024
+        ),
+    )(queries, keys, values, cotangent)
+
+
 def solution(mesh):
     placed = (
         P(("groups", "ctx"), None),

time: 138 us -> 30.2 us (0.22)
  waiting for transfers between devices: 49.7 us -> 0 us
  matrix products: 41.4 us -> 0 us
  Pallas kernels: 0 us -> 23.2 us
  other arithmetic: 15.7 us -> 0 us
  local copies, waits for them, and re-layouts: 19.4 us -> 6.23 us
  starting transfers between devices: 9.18 us -> 0 us
    ppermute x8 -> x0, waiting for transfers between devices: 49.7 us -> none  [swapped(): return lax.ppermute(value, axis, pairs)]
    dot_general x120 -> x0, matrix products: 41.4 us -> none  [the longest x20 11.9 us: attend_sets(): jnp.einsum('gsk,gkd->gsd', s_group, key_parts[set_index], preferred_eleme...]
    pallas_call x0 -> x1, Pallas kernels: none -> 23.2 us  [per_device(): pl.pallas_call(functools.partial(exchange_kernel, levels), out_shape=(fla...]
    ppermute x8 -> x0, starting transfers between devices: 9.18 us -> none  [swapped(): return lax.ppermute(value, axis, pairs)]
    convert_element_type x14 -> x0, other arithmetic: 7.87 us -> none  [the longest x3 5.74 us: pool_rows(): return ((widened[:, 0] + widened[:, 1]) * ROOT_HALF).astype(jnp.bfloat16)]
    convert_element_type x3 -> x0, local copies, waits for them, and re-layouts: 5.04 us -> none  [pool_rows(): pairs.astype(jnp.float32).reshape(pairs.shape[0] // 2, 2, pairs.shape[1])]
    select_n x18 -> x0, local copies, waits for them, and re-layouts: 4.39 us -> none  [the longest x9 2.2 us: per_device(): kept = jnp.where(upper, upper_half, lower_half)]
    add x3 -> x0, other arithmetic: 3.9 us -> none  [per_device(): outgoing = outgoing + jnp.where(upper, lower_half, upper_half)]
  transfers between devices with their start and end apart: 8 -> 0, of which waited for: 6 -> 0; matrix products, arithmetic and copies ran while one was open for 20% -> 0% of each run, Pallas kernels for 0% -> 0%
where the time goes in v1:
time: 30.2 us; the launch traced here: 30 us
  Pallas kernels  23.2 us (77%)
  local copies, waits for them, and re-layouts  6.23 us (21%)
  between operations  0.65 us (2%)
    pallas_call x1, Pallas kernels, per_device(): pl.pallas_call(functools.partial(exchange_kernel, levels), out_shape=(fla...  23.2 us
    unnamed x12, local copies, waits for them, and re-layouts  6.23 us

profile of v1, /device:TPU:1, one launch (start us, length us, event | category | flops | bytes accessed | tf_op | source)
XLA Modules:
  0.0 30.0 jit_solution(13536143276373527656)
XLA Ops:
  0.6 0.0 copy-start
  0.6 0.9 %copy-done = bf16[128,512]{1,0:T(8,128)(2,1)S(1)} copy-done((bf16[128,512]{1,0:T(8,128)(2,1)S(1)}, bf16[128,512]{1,0:T(8,128)(2,1)}, u32[]{:S(2)}) %copy-start) | copy-done | bytes 131096
  1.5 0.0 copy-start.1
  1.5 0.9 %copy-done.1 = bf16[128,512]{1,0:T(8,128)(2,1)S(1)} copy-done((bf16[128,512]{1,0:T(8,128)(2,1)S(1)}, bf16[128,512]{1,0:T(8,128)(2,1)}, u32[]{:S(2)}) %copy-start.1) | copy-done | bytes 131096
  2.4 0.0 copy-start.2
  2.4 0.9 %copy-done.2 = bf16[128,512]{1,0:T(8,128)(2,1)S(1)} copy-done((bf16[128,512]{1,0:T(8,128)(2,1)S(1)}, bf16[128,512]{1,0:T(8,128)(2,1)}, u32[]{:S(2)}) %copy-start.2) | copy-done | bytes 131096
  3.3 0.0 copy-start.3
  3.3 0.9 %copy-done.3 = bf16[128,512]{1,0:T(8,128)(2,1)S(1)} copy-done((bf16[128,512]{1,0:T(8,128)(2,1)S(1)}, bf16[128,512]{1,0:T(8,128)(2,1)}, u32[]{:S(2)}) %copy-start.3) | copy-done | bytes 131096
  4.3 23.2 %shard_map.75 = (bf16[128,512]{1,0:T(8,128)(2,1)S(1)}, bf16[128,512]{1,0:T(8,128)(2,1)S(1)}, bf16[128,512]{1,0:T(8,128)(2,1)S(1)}, bf16[128,512]{1,0:T(8,128)(2,1)S(1)}) custom-call(bf16[128,512]{1,0:T(8,128)(2,1)S(1)} %copy-done, bf16[128,512]{1,0:T(8,128)(2,1)S(1)} %copy-done.1, bf16[128,512]{1,0:T(8,128)(2,1)S(1)} %copy-done.2, bf16[128,512]{1,0:T(8,128)(2,1)S(1)} %copy-done.3), custom_call_target="tpu_custom_call" | custom-call | tf_op jit(solution)/shard_map/pallas_call | solution.py:459
  27.4 0.7 %copy.12 = bf16[128,512]{1,0:T(8,128)(2,1)} copy(bf16[128,512]{1,0:T(8,128)(2,1)S(1)} %get-tuple-element.8) | data formatting | bytes 262144
  28.1 0.7 %copy.13 = bf16[128,512]{1,0:T(8,128)(2,1)} copy(bf16[128,512]{1,0:T(8,128)(2,1)S(1)} %get-tuple-element.9) | data formatting | bytes 262144
  28.7 0.7 %copy.14 = bf16[128,512]{1,0:T(8,128)(2,1)} copy(bf16[128,512]{1,0:T(8,128)(2,1)S(1)} %get-tuple-element.10) | data formatting | bytes 262144
  29.4 0.7 %copy.15 = bf16[128,512]{1,0:T(8,128)(2,1)} copy(bf16[128,512]{1,0:T(8,128)(2,1)S(1)} %get-tuple-element.11) | data formatting | bytes 262144
Async XLA Ops:
  0.6 0.9 %copy-start = (bf16[128,512]{1,0:T(8,128)(2,1)S(1)}, bf16[128,512]{1,0:T(8,128)(2,1)}, u32[]{:S(2)}) copy-start(bf16[128,512]{1,0:T(8,128)(2,1)} %q_ref.1) | copy-start | bytes 393220
  1.5 0.9 %copy-start.1 = (bf16[128,512]{1,0:T(8,128)(2,1)S(1)}, bf16[128,512]{1,0:T(8,128)(2,1)}, u32[]{:S(2)}) copy-start(bf16[128,512]{1,0:T(8,128)(2,1)} %k_ref.1) | copy-start | bytes 393220
  2.4 0.9 %copy-start.2 = (bf16[128,512]{1,0:T(8,128)(2,1)S(1)}, bf16[128,512]{1,0:T(8,128)(2,1)}, u32[]{:S(2)}) copy-start(bf16[128,512]{1,0:T(8,128)(2,1)} %v_ref.1) | copy-start | bytes 393220
  3.3 0.9 %copy-start.3 = (bf16[128,512]{1,0:T(8,128)(2,1)S(1)}, bf16[128,512]{1,0:T(8,128)(2,1)}, u32[]{:S(2)}) copy-start(bf16[128,512]{1,0:T(8,128)(2,1)} %d_ref.1) | copy-start | bytes 393220

commit v2 on v1

--- a/solution.py
+++ b/solution.py
@@ -175,8 +175,8 @@
     return (attended, query_grad.astype(jnp.bfloat16), key_grad, value_grad)
 
 
-def chunk_slot(level, member):
-    return (1 << level) - 2 + member
+def chunk_slot(level, head, member):
+    return 2 * ((1 << level) - 2) + head * (1 << level) + member
 
 
 def contract(left, right, left_dim, right_dim):
@@ -187,26 +187,32 @@
 
 def exchange_kernel(
     levels,
-    q_ref,
-    k_ref,
-    v_ref,
-    d_ref,
+    q_hbm,
+    k_hbm,
+    v_hbm,
+    d_hbm,
     att_ref,
     dq_ref,
     dk_ref,
     dv_ref,
+    k_ref,
+    v_ref,
+    q_ref,
+    d_ref,
     wide,
+    pairs,
+    queried,
     pooled,
-    q_all,
-    d_all,
+    queries_all,
     kv_all,
     grad_out,
     grad_in,
     near_out,
     near_in,
-    att_out,
-    dq_out,
+    result_out,
+    result_in,
     spread,
+    load_sem,
     pool_send,
     pool_recv,
     near_send,
@@ -241,11 +247,24 @@
             barrier, inc=1, device_id={"ctx": other}, device_id_type=pl.DeviceIdType.MESH
         )
 
+    loads = [
+        pltpu.make_async_copy(src, dst, load_sem.at[i])
+        for i, (src, dst) in enumerate(
+            [(k_hbm, k_ref), (v_hbm, v_ref), (q_hbm, q_ref), (d_hbm, d_ref)]
+        )
+    ]
+    for load in loads:
+        load.start()
+    for load in loads[:2]:
+        load.wait()
+
     for c in range(2):
         for part in range(4):
-            src = k_ref if part < 2 else v_ref
-            low_col = c * half + part % 2 * HEAD_DIM
-            wide[c * 4 + part] = src[:, low_col : low_col + HEAD_DIM].astype(jnp.float32)
+            src = v_ref if part % 2 else k_ref
+            low_col = c * half + part // 2 * HEAD_DIM
+            column = src[:, low_col : low_col + HEAD_DIM]
+            pairs[c, part // 2, :, part % 2 * HEAD_DIM : (part % 2 + 1) * HEAD_DIM] = column
+            wide[c * 4 + part] = column.astype(jnp.float32)
     for level in range(1, levels):
         rows = BLOCK >> level
         base = BLOCK - 2 * rows
@@ -255,12 +274,18 @@
                 even = column[pl.ds(0, rows, stride=2), :]
                 odd = column[pl.ds(1, rows, stride=2), :]
                 low = ((even + odd) * ROOT_HALF).astype(jnp.bfloat16)
-                pooled[c, base : base + rows, part * HEAD_DIM : (part + 1) * HEAD_DIM] = low
+                low_col = part % 2 * HEAD_DIM
+                pooled[c, part // 2, base : base + rows, low_col : low_col + HEAD_DIM] = low
                 if level + 1 < levels:
                     column[0:rows, :] = low.astype(jnp.float32)
+    for load in loads[2:]:
+        load.wait()
+    for c in range(2):
+        queried[c, :, :half] = q_ref[:, c * half : (c + 1) * half]
+        queried[c, :, half:] = d_ref[:, c * half : (c + 1) * half]
     pl.semaphore_wait(barrier, count - 1)
 
-    def pool_copy(level, member):
+    def pool_copy(level, head, member):
         rows = BLOCK >> level
         base = BLOCK - 2 * rows
         size = 1 << level
@@ -268,48 +293,47 @@
         group = lax.div(me, size)
         partner = group + 1 - 2 * lax.rem(group, 2)
         return remote(
-            pooled.at[member % 2, pl.ds(base, rows), :],
-            kv_all.at[pl.ds(pl.multiple_of(BLOCK * (level + 1) + mine * rows, rows), rows), :],
-            pool_send.at[chunk_slot(level, member)],
-            pool_recv.at[chunk_slot(level, 0) + mine],
+            pooled.at[member % 2, head, pl.ds(base, rows), :],
+            kv_all.at[head, pl.ds(pl.multiple_of(BLOCK * (level + 1) + mine * rows, rows), rows), :],
+            pool_send.at[chunk_slot(level, head, member)],
+            pool_recv.at[chunk_slot(level, head, 0) + mine],
             partner * size + member,
         )
 
-    def pool_arrival(level, member):
+    def pool_arrival(level, head, member):
         rows = BLOCK >> level
         base = BLOCK - 2 * rows
         return remote(
-            pooled.at[0, pl.ds(base, rows), :],
-            kv_all.at[pl.ds(BLOCK * (level + 1) + member * rows, rows), :],
-            pool_send.at[chunk_slot(level, member)],
-            pool_recv.at[chunk_slot(level, member)],
+            pooled.at[0, head, pl.ds(base, rows), :],
+            kv_all.at[head, pl.ds(BLOCK * (level + 1) + member * rows, rows), :],
+            pool_send.at[chunk_slot(level, head, member)],
+            pool_recv.at[chunk_slot(level, head, member)],
             sibling,
         )
 
     own_rows = pl.ds(pl.multiple_of(core * BLOCK, BLOCK), BLOCK)
     sib_rows = pl.ds(pl.multiple_of(BLOCK - core * BLOCK, BLOCK), BLOCK)
+    near_pairs = [
+        (queried.at[1 - core], queries_all.at[own_rows, :]),
+        (pairs.at[1 - core], kv_all.at[:, own_rows, :]),
+    ]
     near = [
-        remote(src.at[:, sib_cols], dst, near_send.at[i], near_recv.at[i], sibling)
-        for i, (src, dst) in enumerate(
-            [
-                (q_ref, q_all.at[own_rows, :]),
-                (k_ref, kv_all.at[own_rows, pl.ds(0, half)]),
-                (v_ref, kv_all.at[own_rows, pl.ds(half, half)]),
-                (d_ref, d_all.at[own_rows, :]),
-            ]
-        )
+        remote(src, dst, near_send.at[i], near_recv.at[i], sibling)
+        for i, (src, dst) in enumerate(near_pairs)
     ]
     pool_copies = [
-        pool_copy(level, member) for level in reversed(range(1, levels)) for member in range(1 << level)
+        pool_copy(level, head, member)
+        for head in range(2)
+        for level in reversed(range(1, levels))
+        for member in range(1 << level)
     ]
     for copy in near:
         copy.start()
     for copy in pool_copies:
         copy.start()
-    q_all[own_rows, :] = q_ref[:, own_cols]
-    d_all[own_rows, :] = d_ref[:, own_cols]
-    kv_all[own_rows, 0:half] = k_ref[:, own_cols]
-    kv_all[own_rows, half : 2 * half] = v_ref[:, own_cols]
+    queries_all[own_rows, :] = queried[core]
+    for h in range(2):
+        kv_all[h, own_rows, :] = pairs[core, h]
     for copy in near:
         copy.wait_recv()
 
@@ -317,52 +341,55 @@
     score_scale = HEAD_DIM ** (-0.5)
     scores = [[], []]
     dprobs = [[], []]
-    q_heads = [q_all[:, h * HEAD_DIM : (h + 1) * HEAD_DIM] for h in range(2)]
-    d_heads = [d_all[:, h * HEAD_DIM : (h + 1) * HEAD_DIM] for h in range(2)]
+    q_heads = [queries_all[:, h * HEAD_DIM : (h + 1) * HEAD_DIM] for h in range(2)]
+    d_heads = [queries_all[:, half + h * HEAD_DIM : half + (h + 1) * HEAD_DIM] for h in range(2)]
 
     def k_part(index, h):
         low, rows = segments[index]
-        return kv_all[low : low + rows, h * HEAD_DIM : (h + 1) * HEAD_DIM]
+        return kv_all[h, low : low + rows, :HEAD_DIM]
 
     def v_part(index, h):
         low, rows = segments[index]
-        return kv_all[low : low + rows, half + h * HEAD_DIM : half + (h + 1) * HEAD_DIM]
-
-    for index in range(levels):
-        if index > 0:
-            for member in range(1 << index):
-                pool_arrival(index, member).wait_recv()
-        for h in range(2):
-            scores[h].append(contract(q_heads[h], k_part(index, h), 1, 1) * score_scale)
-            dprobs[h].append(contract(d_heads[h], v_part(index, h), 1, 1))
-
-    def grad_copy(level, member):
+        return kv_all[h, low : low + rows, HEAD_DIM:]
+
+    def products(index, h):
+        scores[h].append(contract(q_heads[h], k_part(index, h), 1, 1) * score_scale)
+        dprobs[h].append(contract(d_heads[h], v_part(index, h), 1, 1))
+
+    for h in range(2):
+        products(0, h)
+
+    def grad_copy(level, head, member):
         rows = BLOCK >> level
         size = 1 << level
         mine = lax.rem(me, size)
         group = lax.div(me, size)
         partner = group + 1 - 2 * lax.rem(group, 2)
         return remote(
-            grad_out.at[level - 1, pl.ds(member * rows, rows), :],
-            grad_in.at[level - 1, pl.ds(pl.multiple_of(mine * rows, rows), rows), :],
-            grad_send.at[chunk_slot(level, member)],
-            grad_recv.at[chunk_slot(level, 0) + mine],
+            grad_out.at[level - 1, head, pl.ds(member * rows, rows), :],
+            grad_in.at[level - 1, head, pl.ds(pl.multiple_of(mine * rows, rows), rows), :],
+            grad_send.at[chunk_slot(level, head, member)],
+            grad_recv.at[chunk_slot(level, head, 0) + mine],
             partner * size + member,
         )
 
-    def grad_arrival(level, member):
+    def grad_arrival(level, head, member):
         rows = BLOCK >> level
         return remote(
-            grad_out.at[level - 1, pl.ds(member * rows, rows), :],
-            grad_in.at[level - 1, pl.ds(member * rows, rows), :],
-            grad_send.at[chunk_slot(level, member)],
-            grad_recv.at[chunk_slot(level, member)],
+            grad_out.at[level - 1, head, pl.ds(member * rows, rows), :],
+            grad_in.at[level - 1, head, pl.ds(member * rows, rows), :],
+            grad_send.at[chunk_slot(level, head, member)],
+            grad_recv.at[chunk_slot(level, head, member)],
             sibling,
         )
 
-    near_grads = []
+    grad_copies = []
     for h in range(2):
         low_col = h * HEAD_DIM
+        for index in range(1, levels):
+            for member in range(1 << index):
+                pool_arrival(index, h, member).wait_recv()
+            products(index, h)
         peak = jnp.max(scores[h][0], axis=1, keepdims=True)
         for part in scores[h][1:]:
             peak = jnp.maximum(peak, jnp.max(part, axis=1, keepdims=True))
@@ -377,7 +404,7 @@
         for index in range(1, levels):
             output = output + contract(probs_low[index], v_part(index, h), 1, 0)
         attended = output.astype(jnp.bfloat16)
-        att_out[:, low_col : low_col + HEAD_DIM] = attended
+        result_out[:, low_col : low_col + HEAD_DIM] = attended
         delta = jnp.sum(
             d_heads[h].astype(jnp.float32) * attended.astype(jnp.float32), axis=1, keepdims=True
         )
@@ -385,66 +412,78 @@
             (score_scale * part * (dpart - delta)).astype(jnp.bfloat16)
             for part, dpart in zip(probs, dprobs[h])
         ]
-        for index in range(1, levels):
-            grad_out[index - 1, :, low_col : low_col + HEAD_DIM] = contract(
+        for index in reversed(range(1, levels)):
+            grad_out[index - 1, h, :, :HEAD_DIM] = contract(
                 dscores[index], q_heads[h], 0, 0
             ).astype(jnp.bfloat16)
-            grad_out[index - 1, :, half + low_col : half + low_col + HEAD_DIM] = contract(
+            grad_out[index - 1, h, :, HEAD_DIM:] = contract(
                 probs_low[index], d_heads[h], 0, 0
             ).astype(jnp.bfloat16)
-        near_grads.append((dscores, probs_low))
-    grad_copies = [
-        grad_copy(level, member) for level in reversed(range(1, levels)) for member in range(1 << level)
-    ]
-    for copy in grad_copies:
-        copy.start()
-    for h in range(2):
-        low_col = h * HEAD_DIM
-        dscores, probs_low = near_grads[h]
-        near_out[:, low_col : low_col + HEAD_DIM] = contract(dscores[0], q_heads[h], 0, 0).astype(jnp.bfloat16)
-        near_out[:, half + low_col : half + low_col + HEAD_DIM] = contract(
+            for member in range(1 << index):
+                copy = grad_copy(index, h, member)
+                copy.start()
+                grad_copies.append(copy)
+        near_out[h, :, :HEAD_DIM] = contract(dscores[0], q_heads[h], 0, 0).astype(jnp.bfloat16)
+        near_out[h, :, HEAD_DIM:] = contract(
             probs_low[0], d_heads[h], 0, 0
         ).astype(jnp.bfloat16)
         query_total = contract(dscores[0], k_part(0, h), 1, 0)
         for index in range(1, levels):
             query_total = query_total + contract(dscores[index], k_part(index, h), 1, 0)
-        dq_out[:, low_col : low_col + HEAD_DIM] = query_total.astype(jnp.bfloat16)
+        result_out[:, half + low_col : half + low_col + HEAD_DIM] = query_total.astype(jnp.bfloat16)
     back = [
-        remote(near_out.at[sib_rows, :], near_in.at[core], back_send.at[0], back_recv.at[0], sibling),
-        remote(att_out.at[sib_rows, :], att_ref.at[:, own_cols], back_send.at[1], back_recv.at[1], sibling),
-        remote(dq_out.at[sib_rows, :], dq_ref.at[:, own_cols], back_send.at[2], back_recv.at[2], sibling),
+        remote(near_out.at[:, sib_rows, :], near_in.at[core], back_send.at[0], back_recv.at[0], sibling),
+        remote(result_out.at[sib_rows, :], result_in, back_send.at[1], back_recv.at[1], sibling),
     ]
     for copy in back:
         copy.start()
-    near_in[core] = near_out[own_rows, :]
-    att_ref[:, own_cols] = att_out[own_rows, :]
-    dq_ref[:, own_cols] = dq_out[own_rows, :]
-    for level in reversed(range(1, levels)):
-        for member in range(1 << level):
-            grad_arrival(level, member).wait_recv()
+    for h in range(2):
+        near_in[core, h] = near_out[h, own_rows, :]
+    att_ref[:, own_cols] = result_out[own_rows, :half]
+    dq_ref[:, own_cols] = result_out[own_rows, half:]
     back[0].wait_recv()
-    for c in range(2):
-        carried = None
+    for h in range(2):
+        carried = [None, None]
         for level in reversed(range(1, levels)):
             rows = BLOCK >> level
-            for member in range(c, 1 << level, 2):
-                part = grad_in[level - 1, member * rows : (member + 1) * rows, :].astype(jnp.float32)
-                carried = part if carried is None else carried + part
-            carried = carried * ROOT_HALF
-            for part in range(4):
-                column = spread.at[part]
-                piece = carried[:, part * HEAD_DIM : (part + 1) * HEAD_DIM]
-                column[pl.ds(0, rows, stride=2), :] = piece
-                column[pl.ds(1, rows, stride=2), :] = piece
-            carried = jnp.concatenate([spread[part, 0 : 2 * rows, :] for part in range(4)], axis=1)
-        carried = carried + near_in[c].astype(jnp.float32)
-        low = carried.astype(jnp.bfloat16)
-        dk_ref[:, c * half : (c + 1) * half] = low[:, :half]
-        dv_ref[:, c * half : (c + 1) * half] = low[:, half:]
-    for copy in back[1:]:
-        copy.wait_recv()
+            for member in range(1 << level):
+                grad_arrival(level, h, member).wait_recv()
+            for c in range(2):
+                for member in range(c, 1 << level, 2):
+                    part = grad_in[level - 1, h, member * rows : (member + 1) * rows, :].astype(jnp.float32)
+                    carried[c] = part if carried[c] is None else carried[c] + part
+                carried[c] = carried[c] * ROOT_HALF
+                for place in range(2):
+                    column = spread.at[2 * c + place]
+                    piece = carried[c][:, place * HEAD_DIM : (place + 1) * HEAD_DIM]
+                    column[pl.ds(0, rows, stride=2), :] = piece
+                    column[pl.ds(1, rows, stride=2), :] = piece
+                carried[c] = jnp.concatenate(
+                    [spread[2 * c + place, 0 : 2 * rows, :] for place in range(2)], axis=1
+                )
+        for c in range(2):
+            low = (carried[c] + near_in[c, h].astype(jnp.float32)).astype(jnp.bfloat16)
+            low_col = c * half + h * HEAD_DIM
+            dk_ref[:, low_col : low_col + HEAD_DIM] = low[:, :HEAD_DIM]
+            dv_ref[:, low_col : low_col + HEAD_DIM] = low[:, HEAD_DIM:]
+    back[1].wait_recv()
+    att_ref[:, sib_cols] = result_in[:, :half]
+    dq_ref[:, sib_cols] = result_in[:, half:]
     for copy in near + pool_copies + grad_copies + back:
         copy.wait_send()
+
+
+def place_kernel(*refs):
+    sources, results, held, arrive, leave = refs[:4], refs[4:8], refs[8], refs[9], refs[10]
+    inward = [pltpu.make_async_copy(sources[i], held.at[i], arrive.at[i]) for i in range(4)]
+    outward = [pltpu.make_async_copy(held.at[i], results[i], leave.at[i]) for i in range(4)]
+    for copy in inward:
+        copy.start()
+    for first, second in zip(inward, outward):
+        first.wait()
+        second.start()
+    for copy in outward:
+        copy.wait()
 
 
 def per_device(queries, keys, values, cotangent):
@@ -452,41 +491,60 @@
     levels = lax.axis_size("ctx").bit_length() - 1
     if tok_count != BLOCK or levels < 2 or BLOCK >> (levels - 1) < 16:
         return per_device_chained(queries, keys, values, cotangent)
-    chunks = (1 << levels) - 2
+    chunks = 2 * ((1 << levels) - 2)
     half = model_cols // 2
     flat = jax.ShapeDtypeStruct((tok_count, model_cols), jnp.bfloat16)
     vmem = pl.BlockSpec(memory_space=pltpu.VMEM)
-    return pl.pallas_call(
+    results = pl.pallas_call(
         functools.partial(exchange_kernel, levels),
         out_shape=(flat, flat, flat, flat),
-        in_specs=[vmem] * 4,
+        in_specs=[pl.BlockSpec(memory_space=pl.ANY)] * 4,
         out_specs=(vmem,) * 4,
         scratch_shapes=[
+            pltpu.VMEM((BLOCK, model_cols), jnp.bfloat16),
+            pltpu.VMEM((BLOCK, model_cols), jnp.bfloat16),
+            pltpu.VMEM((BLOCK, model_cols), jnp.bfloat16),
+            pltpu.VMEM((BLOCK, model_cols), jnp.bfloat16),
             pltpu.VMEM((8, BLOCK, HEAD_DIM), jnp.float32),
+            pltpu.VMEM((2, 2, BLOCK, half), jnp.bfloat16),
             pltpu.VMEM((2, BLOCK, model_cols), jnp.bfloat16),
-            pltpu.VMEM((2 * BLOCK, half), jnp.bfloat16),
-            pltpu.VMEM((2 * BLOCK, half), jnp.bfloat16),
-            pltpu.VMEM((BLOCK * (levels + 1), model_cols), jnp.bfloat16),
-            pltpu.VMEM((levels - 1, BLOCK, model_cols), jnp.bfloat16),
-            pltpu.VMEM((levels - 1, BLOCK, model_cols), jnp.bfloat16),
+            pltpu.VMEM((2, 2, BLOCK, half), jnp.bfloat16),
             pltpu.VMEM((2 * BLOCK, model_cols), jnp.bfloat16),
-            pltpu.VMEM((2, BLOCK, model_cols), jnp.bfloat16),
-            pltpu.VMEM((2 * BLOCK, half), jnp.bfloat16),
-            pltpu.VMEM((2 * BLOCK, half), jnp.bfloat16),
+            pltpu.VMEM((2, BLOCK * (levels + 1), half), jnp.bfloat16),
+            pltpu.VMEM((levels - 1, 2, BLOCK, half), jnp.bfloat16),
+            pltpu.VMEM((levels - 1, 2, BLOCK, half), jnp.bfloat16),
+            pltpu.VMEM((2, 2 * BLOCK, half), jnp.bfloat16),
+            pltpu.VMEM((2, 2, BLOCK, half), jnp.bfloat16),
+            pltpu.VMEM((2 * BLOCK, model_cols), jnp.bfloat16),
+            pltpu.VMEM((BLOCK, model_cols), jnp.bfloat16),
             pltpu.VMEM((4, BLOCK, HEAD_DIM), jnp.float32),
-            pltpu.SemaphoreType.DMA((chunks,)),
-            pltpu.SemaphoreType.DMA((chunks,)),
-            pltpu.SemaphoreType.DMA((4,)),
             pltpu.SemaphoreType.DMA((4,)),
             pltpu.SemaphoreType.DMA((chunks,)),
             pltpu.SemaphoreType.DMA((chunks,)),
-            pltpu.SemaphoreType.DMA((3,)),
-            pltpu.SemaphoreType.DMA((3,)),
+            pltpu.SemaphoreType.DMA((2,)),
+            pltpu.SemaphoreType.DMA((2,)),
+            pltpu.SemaphoreType.DMA((chunks,)),
+            pltpu.SemaphoreType.DMA((chunks,)),
+            pltpu.SemaphoreType.DMA((2,)),
+            pltpu.SemaphoreType.DMA((2,)),
         ],
         compiler_params=pltpu.CompilerParams(
-            collective_id=0, has_side_effects=True, vmem_limit_bytes=32 * 1024 * 1024
+            collective_id=0, has_side_effects=True, vmem_limit_bytes=56 * 1024 * 1024
         ),
     )(queries, keys, values, cotangent)
+    anywhere = pl.BlockSpec(memory_space=pl.ANY)
+    return pl.pallas_call(
+        place_kernel,
+        out_shape=(flat, flat, flat, flat),
+        in_specs=[anywhere] * 4,
+        out_specs=(anywhere,) * 4,
+        scratch_shapes=[
+            pltpu.VMEM((4, tok_count, model_cols), jnp.bfloat16),
+            pltpu.SemaphoreType.DMA((4,)),
+            pltpu.SemaphoreType.DMA((4,)),
+        ],
+        compiler_params=pltpu.CompilerParams(vmem_limit_bytes=56 * 1024 * 1024),
+    )(*results)
 
 
 def solution(mesh):

time: 30.2 us -> 24.1 us (0.80)
  local copies, waits for them, and re-layouts: 6.23 us -> 0 us
    unnamed x12 -> x0, local copies, waits for them, and re-layouts: 6.23 us -> none
    pallas_call x0 -> x1, Pallas kernels: none -> 1.82 us  [per_device(): pl.pallas_call(place_kernel, out_shape=(flat, flat, flat, flat), in_specs...]
    pallas_call x1, Pallas kernels: 23.2 us -> 21.5 us  [per_device(): pl.pallas_call(functools.partial(exchange_kernel, levels), out_shape=(fla...]
where the time goes in v2:
time: 24.1 us; the launch traced here: 24 us
  Pallas kernels  23.3 us (97%)
  between operations  0.64 us (3%)
    pallas_call x1, Pallas kernels, per_device(): pl.pallas_call(functools.partial(exchange_kernel, levels), out_shape=(fla...  21.5 us
    pallas_call x1, Pallas kernels, per_device(): pl.pallas_call(place_kernel, out_shape=(flat, flat, flat, flat), in_specs...  1.82 us

profile of v2, /device:TPU:1, one launch (start us, length us, event | category | flops | bytes accessed | tf_op | source)
XLA Modules:
  0.0 24.0 jit_solution(5401326213857155533)
XLA Ops:
  0.6 21.5 %shard_map.75 = (bf16[128,512]{1,0:T(8,128)(2,1)}, bf16[128,512]{1,0:T(8,128)(2,1)}, bf16[128,512]{1,0:T(8,128)(2,1)}, bf16[128,512]{1,0:T(8,128)(2,1)}) custom-call(bf16[128,512]{1,0:T(8,128)(2,1)} %q_hbm.1, bf16[128,512]{1,0:T(8,128)(2,1)} %k_hbm.1, bf16[128,512]{1,0:T(8,128)(2,1)} %v_hbm.1, bf16[128,512]{1,0:T(8,128)(2,1)} %d_hbm.1), custom_call_target="tpu_custom_call" | custom-call | tf_op jit(solution)/shard_map/pallas_call | solution.py:498
  22.2 1.8 %shard_map.76 = (bf16[128,512]{1,0:T(8,128)(2,1)}, bf16[128,512]{1,0:T(8,128)(2,1)}, bf16[128,512]{1,0:T(8,128)(2,1)}, bf16[128,512]{1,0:T(8,128)(2,1)}) custom-call(bf16[128,512]{1,0:T(8,128)(2,1)} %get-tuple-element.8.refs_0_, bf16[128,512]{1,0:T(8,128)(2,1)} %get-tuple-element.9.refs_1_, bf16[128,512]{1,0:T(8,128)(2,1)} %get-tuple-element.10.refs_2_, ...), custom_call_target="tpu_custom_call" | custom-call | tf_op jit(solution)/shard_map/pallas_call | solution.py:536

commit v3 on v2

--- a/solution.py
+++ b/solution.py
@@ -191,6 +191,10 @@
     k_hbm,
     v_hbm,
     d_hbm,
+    att_hbm,
+    dq_hbm,
+    dk_hbm,
+    dv_hbm,
     att_ref,
     dq_ref,
     dk_ref,
@@ -213,6 +217,7 @@
     result_in,
     spread,
     load_sem,
+    store_sem,
     pool_send,
     pool_recv,
     near_send,
@@ -315,7 +320,8 @@
     sib_rows = pl.ds(pl.multiple_of(BLOCK - core * BLOCK, BLOCK), BLOCK)
     near_pairs = [
         (queried.at[1 - core], queries_all.at[own_rows, :]),
-        (pairs.at[1 - core], kv_all.at[:, own_rows, :]),
+        (pairs.at[1 - core, 0], kv_all.at[0, own_rows, :]),
+        (pairs.at[1 - core, 1], kv_all.at[1, own_rows, :]),
     ]
     near = [
         remote(src, dst, near_send.at[i], near_recv.at[i], sibling)
@@ -432,8 +438,10 @@
             query_total = query_total + contract(dscores[index], k_part(index, h), 1, 0)
         result_out[:, half + low_col : half + low_col + HEAD_DIM] = query_total.astype(jnp.bfloat16)
     back = [
-        remote(near_out.at[:, sib_rows, :], near_in.at[core], back_send.at[0], back_recv.at[0], sibling),
-        remote(result_out.at[sib_rows, :], result_in, back_send.at[1], back_recv.at[1], sibling),
+        remote(near_out.at[h, sib_rows, :], near_in.at[core, h], back_send.at[h], back_recv.at[h], sibling)
+        for h in range(2)
+    ] + [
+        remote(result_out.at[sib_rows, :], result_in, back_send.at[2], back_recv.at[2], sibling),
     ]
     for copy in back:
         copy.start()
@@ -441,7 +449,19 @@
         near_in[core, h] = near_out[h, own_rows, :]
     att_ref[:, own_cols] = result_out[own_rows, :half]
     dq_ref[:, own_cols] = result_out[own_rows, half:]
-    back[0].wait_recv()
+    back[2].wait_recv()
+    att_ref[:, sib_cols] = result_in[:, :half]
+    dq_ref[:, sib_cols] = result_in[:, half:]
+    stores = [
+        pltpu.make_async_copy(src, dst, store_sem.at[i])
+        for i, (src, dst) in enumerate(
+            [(att_ref, att_hbm), (dq_ref, dq_hbm), (dk_ref, dk_hbm), (dv_ref, dv_hbm)]
+        )
+    ]
+    for store in stores[:2]:
+        store.start()
+    for copy in back[:2]:
+        copy.wait_recv()
     for h in range(2):
         carried = [None, None]
         for level in reversed(range(1, levels)):
@@ -466,9 +486,10 @@
             low_col = c * half + h * HEAD_DIM
             dk_ref[:, low_col : low_col + HEAD_DIM] = low[:, :HEAD_DIM]
             dv_ref[:, low_col : low_col + HEAD_DIM] = low[:, HEAD_DIM:]
-    back[1].wait_recv()
-    att_ref[:, sib_cols] = result_in[:, :half]
-    dq_ref[:, sib_cols] = result_in[:, half:]
+    for store in stores[2:]:
+        store.start()
+    for store in stores:
+        store.wait()
     for copy in near + pool_copies + grad_copies + back:
         copy.wait_send()
 
@@ -494,13 +515,17 @@
     chunks = 2 * ((1 << levels) - 2)
     half = model_cols // 2
     flat = jax.ShapeDtypeStruct((tok_count, model_cols), jnp.bfloat16)
-    vmem = pl.BlockSpec(memory_space=pltpu.VMEM)
+    anywhere = pl.BlockSpec(memory_space=pl.ANY)
     results = pl.pallas_call(
         functools.partial(exchange_kernel, levels),
         out_shape=(flat, flat, flat, flat),
-        in_specs=[pl.BlockSpec(memory_space=pl.ANY)] * 4,
-        out_specs=(vmem,) * 4,
+        in_specs=[anywhere] * 4,
+        out_specs=(anywhere,) * 4,
         scratch_shapes=[
+            pltpu.VMEM((BLOCK, model_cols), jnp.bfloat16),
+            pltpu.VMEM((BLOCK, model_cols), jnp.bfloat16),
+            pltpu.VMEM((BLOCK, model_cols), jnp.bfloat16),
+            pltpu.VMEM((BLOCK, model_cols), jnp.bfloat16),
             pltpu.VMEM((BLOCK, model_cols), jnp.bfloat16),
             pltpu.VMEM((BLOCK, model_cols), jnp.bfloat16),
             pltpu.VMEM((BLOCK, model_cols), jnp.bfloat16),
@@ -519,20 +544,20 @@
             pltpu.VMEM((BLOCK, model_cols), jnp.bfloat16),
             pltpu.VMEM((4, BLOCK, HEAD_DIM), jnp.float32),
             pltpu.SemaphoreType.DMA((4,)),
+            pltpu.SemaphoreType.DMA((4,)),
             pltpu.SemaphoreType.DMA((chunks,)),
             pltpu.SemaphoreType.DMA((chunks,)),
-            pltpu.SemaphoreType.DMA((2,)),
-            pltpu.SemaphoreType.DMA((2,)),
+            pltpu.SemaphoreType.DMA((3,)),
+            pltpu.SemaphoreType.DMA((3,)),
             pltpu.SemaphoreType.DMA((chunks,)),
             pltpu.SemaphoreType.DMA((chunks,)),
-            pltpu.SemaphoreType.DMA((2,)),
-            pltpu.SemaphoreType.DMA((2,)),
+            pltpu.SemaphoreType.DMA((3,)),
+            pltpu.SemaphoreType.DMA((3,)),
         ],
         compiler_params=pltpu.CompilerParams(
             collective_id=0, has_side_effects=True, vmem_limit_bytes=56 * 1024 * 1024
         ),
     )(queries, keys, values, cotangent)
-    anywhere = pl.BlockSpec(memory_space=pl.ANY)
     return pl.pallas_call(
         place_kernel,
         out_shape=(flat, flat, flat, flat),

time: 24.1 us -> 24.1 us (level)
  no operation moved by 1% of the time
where the time goes in v3:
time: 24.1 us; the launch traced here: 24 us
  Pallas kernels  23.3 us (97%)
  between operations  0.64 us (3%)
    pallas_call x1, Pallas kernels, per_device(): pl.pallas_call(functools.partial(exchange_kernel, levels), out_shape=(fla...  21.5 us
    pallas_call x1, Pallas kernels, per_device(): pl.pallas_call(place_kernel, out_shape=(flat, flat, flat, flat), in_specs...  1.82 us

profile of v3, /device:TPU:1, one launch (start us, length us, event | category | flops | bytes accessed | tf_op | source)
XLA Modules:
  0.0 24.0 jit_solution(6837771960389061788)
XLA Ops:
  0.6 21.5 %shard_map.75 = (bf16[128,512]{1,0:T(8,128)(2,1)}, bf16[128,512]{1,0:T(8,128)(2,1)}, bf16[128,512]{1,0:T(8,128)(2,1)}, bf16[128,512]{1,0:T(8,128)(2,1)}) custom-call(bf16[128,512]{1,0:T(8,128)(2,1)} %q_hbm.1, bf16[128,512]{1,0:T(8,128)(2,1)} %k_hbm.1, bf16[128,512]{1,0:T(8,128)(2,1)} %v_hbm.1, bf16[128,512]{1,0:T(8,128)(2,1)} %d_hbm.1), custom_call_target="tpu_custom_call" | custom-call | tf_op jit(solution)/shard_map/pallas_call | solution.py:519
  22.1 1.8 %shard_map.76 = (bf16[128,512]{1,0:T(8,128)(2,1)}, bf16[128,512]{1,0:T(8,128)(2,1)}, bf16[128,512]{1,0:T(8,128)(2,1)}, bf16[128,512]{1,0:T(8,128)(2,1)}) custom-call(bf16[128,512]{1,0:T(8,128)(2,1)} %get-tuple-element.8.refs_0_, bf16[128,512]{1,0:T(8,128)(2,1)} %get-tuple-element.9.refs_1_, bf16[128,512]{1,0:T(8,128)(2,1)} %get-tuple-element.10.refs_2_, ...), custom_call_target="tpu_custom_call" | custom-call | tf_op jit(solution)/shard_map/pallas_call | solution.py:561
